TPU v7x, 512 devices: a whole 4x4x16 slice. The times are simulated.
512 devices in a mesh: blk: 32 (over z_hi, y, x), freq: 16 (over z_lo, core).
Axes of the slice: x: 4, y: 4, z: 16 (z_hi: 2, z_lo: 8; z = z_hi * 8 + z_lo), core: 2. Of those that a mesh axis runs over, the one named last changes fastest.
Arguments:
- traces: bfloat16 [1024, 1024, 1024], P('blk', 'freq'), as said below
- mute: int32 [1024, 1024], P('blk', 'freq'), may hold values from 0 to 127, as said below
- operator: bfloat16 [2, 32, 1024, 1024], P(None, 'freq', 'blk'), may hold values from -0.125 to 0.125
- wavelet: float32 [2, 32], replicated, may hold values from -40 to 40
Outputs:
- gradient: float32 [2, 32, 1024, 1024], P(None, 'freq', 'blk')
Inputs may be any that keep to these rules, and one draw needn't show every extreme that they name: traces[s, r, t] == traces[r, s, t] for all shots s and receivers r (reciprocity). mute[s, r] == mute[r, s]; the largest value is reached in every draw.
All inputs are finite; a program needn't handle non-finite values.
Results may differ from a plain program's by a relative error of at most 0.0041.
Values may be sent and summed in bfloat16 or wider, within the bound.
A program may use at most 64 MiB of HBM per device.

v0:
```python
import math

import jax
import jax.numpy as jnp
from jax import lax
from jax.sharding import PartitionSpec as P

LOW_FREQ = 8


def band_table(samples, count):
    times = jnp.arange(samples, dtype=jnp.int32)
    freqs = LOW_FREQ + jnp.arange(count, dtype=jnp.int32)
    phase = times[:, None] * freqs[None, :] % samples
    angle = phase.astype(jnp.float32) * (2.0 * math.pi / samples)
    factor = 1.0 / math.sqrt(samples)
    return jnp.concatenate([jnp.cos(angle) * factor, -jnp.sin(angle) * factor], axis=1).astype(
        jnp.bfloat16
    )


def batched(left, right):
    return jnp.einsum("fmc,fcn->fmn", left, right, preferred_element_type=jnp.float32)


def add_operator(spectra, piece):
    real_part = batched(spectra[0], piece[0]) - batched(spectra[1], piece[1])
    imag_part = batched(spectra[0], piece[1]) + batched(spectra[1], piece[0])
    return jnp.stack([real_part, imag_part])


def add_residual(spectra, piece):
    real_part = batched(spectra[0], piece[0]) + batched(spectra[1], piece[1])
    imag_part = batched(spectra[0], piece[1]) - batched(spectra[1], piece[0])
    return jnp.stack([real_part, imag_part])


def residual_of(spec_re, spec_im, op_re, op_im, wave_re, wave_im, conv_re, conv_im):
    res_re = spec_re - (wave_re * op_re - wave_im * op_im) + conv_re
    res_im = spec_im - (wave_re * op_im + wave_im * op_re) + conv_im
    return jnp.stack([res_re, res_im]).astype(jnp.bfloat16)


def gradient_of(correlated, resid, wave_re, wave_im, factor):
    rre = resid[0].astype(jnp.float32)
    rim = resid[1].astype(jnp.float32)
    grad_re = (correlated[0] - (wave_re * rre + wave_im * rim)) * factor
    grad_im = (correlated[1] - (wave_re * rim - wave_im * rre)) * factor
    return jnp.stack([grad_re, grad_im])


def cycle_evaluate(spectra, operator, wave_re, wave_im, factor):
    convolved = add_operator(spectra, lax.all_gather(operator, "blk", axis=2, tiled=True))
    resid = residual_of(
        spectra[0].astype(jnp.float32),
        spectra[1].astype(jnp.float32),
        operator[0].astype(jnp.float32),
        operator[1].astype(jnp.float32),
        wave_re,
        wave_im,
        convolved[0],
        convolved[1],
    )
    correlated = add_residual(spectra, lax.all_gather(resid, "blk", axis=2, tiled=True))
    return gradient_of(correlated, resid, wave_re, wave_im, factor)


def evaluate(spectra, operator, wavelet, factor):
    wave_re = wavelet[0][:, None, None]
    wave_im = wavelet[1][:, None, None]
    return cycle_evaluate(spectra, operator, wave_re, wave_im, factor)


def body(traces, mute, operator, wavelet):
    shot_rows, recv_cols, samples = traces.shape
    per_owner = operator.shape[1]
    band = per_owner * lax.axis_size("freq")
    times = jnp.arange(samples, dtype=jnp.int32)
    muted = jnp.where(times[None, None, :] >= mute[:, :, None], traces, jnp.zeros_like(traces))
    table = band_table(samples, band)
    local_spec = lax.dot_general(
        table, muted, (((0,), (2,)), ((), ())), preferred_element_type=jnp.float32
    )
    local_spec = local_spec.astype(jnp.bfloat16).reshape(2, band, shot_rows, recv_cols)
    spectra = lax.all_to_all(local_spec, "freq", split_axis=1, concat_axis=3, tiled=True)
    own_wave = lax.dynamic_slice_in_dim(wavelet, lax.axis_index("freq") * per_owner, per_owner, 1)
    factor = 1.0 / math.sqrt(spectra.shape[3])
    return evaluate(spectra, operator, own_wave, factor)


def solution(mesh):
    in_specs = (P("blk", "freq", None), P("blk", "freq"), P(None, "freq", "blk", None), P())
    out_specs = P(None, "freq", "blk", None)
    return jax.shard_map(body, mesh=mesh, in_specs=in_specs, out_specs=out_specs, check_vma=False)
```

profile of v0, /device:TPU:96, one launch (start us, length us, event | category | flops | bytes accessed | tf_op | source)
XLA Modules:
  0.0 546.6 jit_solution(15707287491383791687)
XLA Ops:
  6.5 0.0 copy-start
  6.5 0.0 all-gather.3.cloned.1.call-start
  6.5 0.7 all-gather.3.cloned.1.call-update
  7.3 0.6 multiply_convert_fusion.1
  7.9 4.4 fusion.13
  12.3 0.6 copy.11
  12.8 1.1 reshape.28
  13.9 11.7 %all-to-all-start = ((bf16[16,2,4096]{2,1,0:T(2,128)(2,1)}), bf16[16,2,4096]{2,1,0:T(2,128)(2,1)S(1)}, u32[]{:S(2)}, u32[]{:S(2)}) async-start(bf16[16,2,4096]{2,1,0:T(2,128)(2,1)} %reshape.28), calls=%async_computation | async-start | bytes 524288 | tf_op jit(solution)/shard_map/all_to_all | solution.py:85
  25.7 0.0 all-gather.5.cloned.1.call-start
  25.7 0.0 copy-done
  25.7 0.1 constant_dynamic-slice_fusion
  25.8 18.0 %all-to-all-done = bf16[16,2,4096]{2,1,0:T(2,128)(2,1)S(1)} async-done(((bf16[16,2,4096]{2,1,0:T(2,128)(2,1)}), bf16[16,2,4096]{2,1,0:T(2,128)(2,1)S(1)}, u32[]{:S(2)}, u32[]{:S(2)}) %all-to-all-start) | async-done | bytes 262176 | tf_op jit(solution)/shard_map/all_to_all | solution.py:85
  43.8 0.3 reshape.29
  44.2 0.3 copy.10
  44.6 0.2 squeeze.12
  44.8 0.2 squeeze.14
  45.0 0.0 copy-start.3
  45.0 228.9 %all-gather.3.cloned.1.call-done = bf16[2,2,1024,1024]{3,2,1,0:T(8,128)(2,1)} async-done(((bf16[2,2,32,1024]{3,2,1,0:T(8,128)(2,1)}), bf16[2,2,1024,1024]{3,2,1,0:T(8,128)(2,1)}) %all-gather.3.cloned.1.call-update) | async-done | bytes 8388624 | tf_op jit(solution)/shard_map/all_gather | solution.py:53
  273.9 0.0 copy-start.2
  273.9 3.2 fusion.5
  277.1 3.5 fusion.4
  280.6 0.0 copy-done.3
  280.6 0.0 copy-done.2
  280.6 0.9 fusion.29
  281.4 0.9 fusion.28
  282.3 0.7 pad_maximum_fusion.1
  283.0 0.0 all-gather.5.cloned.1.call-update
  283.1 247.5 %all-gather.5.cloned.1.call-done = bf16[2,2,1024,1024]{3,2,1,0:T(8,128)(2,1)} async-done(((bf16[2,2,32,1024]{3,2,1,0:T(8,128)(2,1)}), bf16[2,2,1024,1024]{3,2,1,0:T(8,128)(2,1)}) %all-gather.5.cloned.1.call-update) | async-done | bytes 8388624 | tf_op jit(solution)/shard_map/all_gather | solution.py:64
  530.5 0.0 copy-start.1
  530.5 3.2 fusion.9
  533.7 3.5 fusion.8
  537.2 0.0 copy-done.1
  537.2 0.9 fusion.19
  538.0 0.9 fusion.23
  538.9 0.8 pad_maximum_fusion
  (3 shorter events, 0.0 us)
Async XLA Ops:
  6.5 19.2 %copy-start = (f32[2,32]{1,0:T(2,128)S(1)}, f32[2,32]{1,0:T(2,128)}, u32[]{:S(2)}) copy-start(f32[2,32]{1,0:T(2,128)} %param.7) | copy-start | bytes 772
  6.5 267.4 %all-gather.3.cloned.1.call-start = ((), (), s32[]{:S(2)}) async-start(), calls=%async_computation.1 | async-start | bytes 8650752 | tf_op jit(solution)/shard_map/all_gather | solution.py:53
  13.9 29.9 %all-to-all-start = ((bf16[16,2,4096]{2,1,0:T(2,128)(2,1)}), bf16[16,2,4096]{2,1,0:T(2,128)(2,1)S(1)}, u32[]{:S(2)}, u32[]{:S(2)}) async-start(bf16[16,2,4096]{2,1,0:T(2,128)(2,1)} %reshape.28), calls=%async_computation | async-start | bytes 524288 | tf_op jit(solution)/shard_map/all_to_all | solution.py:85
  25.7 504.8 %all-gather.5.cloned.1.call-start = ((), (), s32[]{:S(2)}) async-start(), calls=%async_computation.2 | async-start | bytes 8650752 | tf_op jit(solution)/shard_map/all_gather | solution.py:64
  45.0 235.6 %copy-start.3 = (bf16[2,2,32,1024]{3,2,1,0:T(8,128)(2,1)S(1)}, bf16[2,2,32,1024]{3,2,1,0:T(8,128)(2,1)}, u32[]{:S(2)}) copy-start(bf16[2,2,32,1024]{3,2,1,0:T(8,128)(2,1)} %param.6) | copy-start | bytes 786436
  273.9 6.7 %copy-start.2 = (bf16[2,2,1024,1024]{3,2,1,0:T(8,128)(2,1)S(1)}, bf16[2,2,1024,1024]{3,2,1,0:T(8,128)(2,1)}, u32[]{:S(2)}) copy-start(bf16[2,2,1024,1024]{3,2,1,0:T(8,128)(2,1)} %all-gather.3.cloned.1.call-done) | copy-start | bytes 25165828
  530.5 6.7 %copy-start.1 = (bf16[2,2,1024,1024]{3,2,1,0:T(8,128)(2,1)S(1)}, bf16[2,2,1024,1024]{3,2,1,0:T(8,128)(2,1)}, u32[]{:S(2)}) copy-start(bf16[2,2,1024,1024]{3,2,1,0:T(8,128)(2,1)} %all-gather.5.cloned.1.call-done) | copy-start | bytes 25165828
Sparse Core Ops, SparseCore 0:
  11.8 262.0 all-gather.2
  283.2 247.2 all-gather.4
where the time goes:
time: 547 us
  waiting for transfers between devices  495 us (90%)
  matrix products  21.1 us (4%)
  between operations  13.5 us (2%)
  starting transfers between devices  11.8 us (2%)
    all_gather x1, waiting for transfers between devices, cycle_evaluate(): lax.all_gather(resid, 'blk', axis=2, tiled=True)  247 us
    all_gather x1, waiting for transfers between devices, cycle_evaluate(): lax.all_gather(operator, 'blk', axis=2, tiled=True)  229 us
    all_to_all x1, waiting for transfers between devices, body(): lax.all_to_all(local_spec, 'freq', split_axis=1, concat_axis=3, tiled=True)  18 us
    dot_general x8, matrix products, batched(): jnp.einsum('fmc,fcn->fmn', left, right, preferred_element_type=jnp.float32)  16.7 us
    all_to_all x1, starting transfers between devices, body(): lax.all_to_all(local_spec, 'freq', split_axis=1, concat_axis=3, tiled=True)  11.7 us
  transfers between devices with their start and end apart: 3, of which 3 were waited for; matrix products, arithmetic and copies ran while one was open for 1% of the time, Pallas kernels for 0%

commit v1 on v0

v1 whole, which is shorter than its diff:
```python
import functools
import math

import jax
import jax.numpy as jnp
import numpy as np
from jax import lax
from jax.experimental import pallas as pl
from jax.experimental.pallas import tpu as pltpu
from jax.sharding import PartitionSpec as P

LOW_FREQ = 8
MESH = pl.DeviceIdType.MESH
BF16 = jnp.bfloat16
F32 = jnp.float32

OFFSETS = (0, 1, 3, 6, 4)


def div(a, b):
    return lax.div(a, jnp.int32(b))


def rem(a, b):
    return lax.rem(a, jnp.int32(b))


def band_table(samples, count):
    times = np.arange(samples, dtype=np.int64)
    freqs = LOW_FREQ + np.arange(count, dtype=np.int64)
    phase = times[:, None] * freqs[None, :] % samples
    angle = phase.astype(np.float32) * np.float32(2.0 * math.pi / samples)
    factor = np.float32(1.0 / math.sqrt(samples))
    table = np.concatenate([np.cos(angle) * factor, -np.sin(angle) * factor], axis=1)
    return np.ascontiguousarray(table.T).astype(jnp.bfloat16)


def swap(x):
    return pltpu.roll(x, 64, 1)


def low_half(rows):
    return lax.broadcasted_iota(jnp.int32, (rows, 128), 1) < 64


def kernel(
    table, traces, mute, oper, wave, got,
    tr, zs, zb, pin, pk, xs, xp, w, y, res, gs,
    tr_sem, zsend, zrecv, xsend, xrecv, gsend, grecv, psend, precv,
):
    b = lax.axis_index("blk").astype(jnp.int32)
    f = lax.axis_index("freq").astype(jnp.int32)
    h, xy = div(b, 16), rem(b, 16)
    yy, xx = div(xy, 4), rem(xy, 4)
    l, core = div(f, 2), rem(f, 2)
    z = h * 8 + l
    u = h * 4 + yy
    d = rem(l - u + 8, 8)
    kept = (d == 0) | (d == 1) | (d == 3) | (d == 6) | ((d == 4) & (h == 0))
    slot = jnp.where(d == 1, 1, 0) + jnp.where(d == 3, 2, 0) + jnp.where(d == 6, 3, 0) + jnp.where(d == 4, 4, 0) + 5 * h
    far = rem(l + 4, 8)
    far_f = far * 2 + core
    part = rem(1 + h + div(l, 4), 2)
    mine = far * 4 + core * 2 + part

    def load(ch):
        return pltpu.make_async_copy(traces.at[pl.ds(8 * ch, 8)], tr.at[pl.ds(8 * ch, 8)], tr_sem.at[ch])

    @pl.when(kept)
    def _():
        for ch in range(4):
            load(ch).start()

    barrier = pltpu.get_barrier_semaphore()
    me = z * 2 + core

    def ring_of(i):
        t = rem(me + i, 32)
        to_z, to_core = div(t, 2), rem(t, 2)
        to_h, to_l = div(to_z, 8), rem(to_z, 8)
        return to_h, to_l, to_core

    def greet_ring(i, carry):
        to_h, to_l, to_core = ring_of(i)
        pl.semaphore_signal(barrier, inc=1, device_id=(to_h * 16 + xy, to_l * 2 + to_core), device_id_type=MESH)
        return carry

    def greet_far(i, carry):
        pl.semaphore_signal(barrier, inc=1, device_id=(i, far_f), device_id_type=MESH)
        return carry

    lax.fori_loop(1, 32, greet_ring, 0)
    lax.fori_loop(0, 32, greet_far, 0)

    def near(dy, dx):
        return h * 16 + rem(yy + dy + 4, 4) * 4 + rem(xx + dx + 4, 4)

    for dy, dx in ((0, 1), (0, -1), (1, 0), (-1, 0)):
        pl.semaphore_signal(barrier, inc=1, device_id=(near(dy, dx), f), device_id_type=MESH)

    lo32 = low_half(32)
    for a in range(2):
        for m in range(8):
            re = oper[0, a, :, 128 * m : 128 * m + 128].astype(F32)
            im = oper[1, a, :, 128 * m : 128 * m + 128].astype(F32)
            xs[a, 2 * m] = jnp.where(lo32, re, swap(im)).astype(BF16)
            xs[a, 2 * m + 1] = jnp.where(lo32, swap(re), im).astype(BF16)

    @pl.when(kept)
    def _():
        eye = (lax.broadcasted_iota(jnp.int32, (64, 64), 0) == lax.broadcasted_iota(jnp.int32, (64, 64), 1)).astype(F32)
        ones = jnp.ones((64, 128), BF16)
        lane = lax.broadcasted_iota(jnp.int32, (512, 128), 1).astype(F32)
        for ch in range(4):
            starts = [
                (eye * mute[8 * ch + s : 8 * ch + s + 1, :].astype(F32)).astype(BF16) for s in range(8)
            ]
            first = jnp.dot(jnp.concatenate(starts, axis=0), ones, preferred_element_type=F32)
            load(ch).wait()
            head = tr[8 * ch : 8 * ch + 8, :, 0:128].astype(F32).reshape(512, 128)
            head = jnp.where(lane >= first, head, 0.0).astype(BF16)
            tr[8 * ch : 8 * ch + 8, :, 0:128] = head.reshape(8, 64, 128)
            spec = lax.dot_general(
                table[...], tr[8 * ch : 8 * ch + 8].reshape(512, 1024), (((1,), (1,)), ((), ())),
                preferred_element_type=F32,
            )
            for p in range(4):
                re = spec[0:32, 128 * p : 128 * p + 128]
                im = spec[32:64, 128 * p : 128 * p + 128]
                even = jnp.where(lo32, re, swap(im))
                odd = jnp.where(lo32, swap(re), im)
                s = 8 * ch + 2 * p
                for jt in range(4):
                    zs[pl.ds(jt * 256 + s, 8, stride=32), :] = even[8 * jt : 8 * jt + 8]
                    zs[pl.ds(jt * 256 + s + 1, 8, stride=32), :] = odd[8 * jt : 8 * jt + 8]
        zb[...] = zs[...].astype(BF16)

    pl.semaphore_wait(barrier, 67)

    def freq_of(to_h, to_l, to_core):
        return rem(to_l + 4, 8) * 4 + to_core * 2 + rem(1 + to_h + div(to_l, 4), 2)

    @pl.when(kept)
    def _():
        own = pltpu.make_async_copy(
            zb.at[pl.ds(pl.multiple_of(mine * 32, 32), 32)], pin.at[slot * 2 + core], zrecv
        )
        own.start()

        def send(i, carry):
            to_h, to_l, to_core = ring_of(i)
            j = freq_of(to_h, to_l, to_core)
            pltpu.make_async_remote_copy(
                src_ref=zb.at[pl.ds(pl.multiple_of(j * 32, 32), 32)],
                dst_ref=pin.at[slot * 2 + core],
                send_sem=zsend,
                recv_sem=zrecv,
                device_id=(to_h * 16 + xy, to_l * 2 + to_core),
                device_id_type=MESH,
            ).start()
            return carry

        lax.fori_loop(1, 32, send, 0)

    def send_oper(i, carry):
        a, to_xy = rem(i, 2), rem(xy + div(i, 2), 16)
        to_h = rem(a + 1 + div(far, 4), 2)
        pltpu.make_async_remote_copy(
            src_ref=xs.at[a, to_xy],
            dst_ref=xp.at[pl.ds(pl.multiple_of(b * 32, 32), 32)],
            send_sem=xsend,
            recv_sem=xrecv,
            device_id=(to_h * 16 + to_xy, far_f),
            device_id_type=MESH,
        ).start()
        return carry

    lax.fori_loop(0, 32, send_oper, 0)

    pltpu.make_async_copy(pin, pin, zrecv).wait()
    for k in range(9):
        left, right = pin[2 * k].astype(F32), pin[2 * k + 1].astype(F32)
        pk[xy, 2 * k] = jnp.where(lo32, left, swap(right)).astype(BF16)
        pk[xy, 2 * k + 1] = jnp.where(lo32, swap(left), right).astype(BF16)

    def place(axis, first, second):
        return (second, first) if axis == 0 else (first, second)

    def owner(axis, first, second):
        dy, dx = place(axis, first, second)
        return rem(yy + dy + 4, 4) * 4 + rem(xx + dx + 4, 4)

    def copy(axis, ring, step, panel, start, size, sem):
        dy, dx = place(axis, *((step, 0) if ring == 0 else (0, step)))
        rows = pk.at[owner(axis, *panel), pl.ds(start, size)]
        return pltpu.make_async_remote_copy(
            src_ref=rows, dst_ref=rows, send_sem=psend, recv_sem=precv.at[axis * 20 + sem],
            device_id=(near(dy, dx), f), device_id_type=MESH,
        )

    def arrived(axis, panel, start, size, sem):
        rows = pk.at[owner(axis, *panel), pl.ds(start, size)]
        pltpu.make_async_copy(rows, rows, precv.at[axis * 20 + sem]).wait()

    spans = ((0, 10, 5), (10, 8, 4))

    def out_second(axis, q, at):
        start, size, _ = spans[axis]
        copy(axis, 1, 1, (q, 0), start, size, 4 + 4 * at).start()
        copy(axis, 1, -1, (q, 0), start, size, 5 + 4 * at).start()

    for axis in range(2):
        start, size, half = spans[axis]
        copy(axis, 0, 1, (0, 0), start, size, 0).start()
        copy(axis, 0, -1, (0, 0), start, size, 1).start()
    for axis in range(2):
        out_second(axis, 0, 0)
    for axis in range(2):
        start, size, half = spans[axis]
        arrived(axis, (-1, 0), start, size, 0)
        copy(axis, 0, 1, (-1, 0), start, half, 2).start()
        arrived(axis, (1, 0), start, size, 1)
        copy(axis, 0, -1, (1, 0), start + half, half, 3).start()
    for axis in range(2):
        out_second(axis, -1, 1)
        out_second(axis, 1, 2)
    for axis in range(2):
        start, size, half = spans[axis]
        arrived(axis, (2, 0), start, half, 2)
        arrived(axis, (2, 0), start + half, half, 3)
        out_second(axis, 2, 3)
    for at, q in enumerate((0, -1, 1, 2)):
        for axis in range(2):
            start, size, half = spans[axis]
            arrived(axis, (q, -1), start, size, 4 + 4 * at)
            copy(axis, 1, 1, (q, -1), start, half, 6 + 4 * at).start()
            arrived(axis, (q, 1), start, size, 5 + 4 * at)
            copy(axis, 1, -1, (q, 1), start + half, half, 7 + 4 * at).start()
    for at, q in enumerate((0, -1, 1, 2)):
        for axis in range(2):
            start, size, half = spans[axis]
            arrived(axis, (q, 2), start, half, 6 + 4 * at)
            arrived(axis, (q, 2), start + half, half, 7 + 4 * at)

    for row in range(8):
        for k in range(5 if row < 4 else 4):
            col = (row + OFFSETS[k]) % 8
            for c in range(2):
                tile = jnp.concatenate(
                    [pk[4 * (row % 4) + x, 2 * (k + 5 * (row // 4)) + c] for x in range(4)], axis=0
                )
                w[128 * row : 128 * row + 128, 256 * col + 128 * c : 256 * col + 128 * c + 128] = tile
                if col != row:
                    w[128 * col : 128 * col + 128, 256 * row + 128 * c : 256 * row + 128 * c + 128] = tile.T

    pltpu.make_async_copy(xp, xp, xrecv).wait()
    lo = low_half(128)
    lane = lax.broadcasted_iota(jnp.int32, (128, 128), 1)
    row_at = lax.broadcasted_iota(jnp.int32, (128, 128), 0)
    for v in range(8):
        x = xp[128 * v : 128 * v + 128].astype(F32)
        sx = swap(x)
        y[256 * v : 256 * v + 128, 0:128] = x.astype(BF16)
        y[256 * v + 128 : 256 * v + 256, 0:128] = jnp.where(lo, -sx, sx).astype(BF16)
        here = row_at + (128 * v - 64 * xy)
        y[256 * v : 256 * v + 128, 128:256] = jnp.where(lo & (lane == here), 1.0, 0.0).astype(BF16)
        y[256 * v + 128 : 256 * v + 256, 128:256] = jnp.where(
            (lane >= 64) & (lane - 64 == here), 1.0, 0.0
        ).astype(BF16)
    qr, qi = wave[0, mine], wave[1, mine]
    lo256 = low_half(256)
    for m in range(4):
        rows = slice(256 * m, 256 * m + 256)
        conv = jnp.dot(w[rows], y[...], preferred_element_type=F32)
        x = xp[rows].astype(F32)
        sx = swap(x)
        r = conv[:, 128:256] - (qr * x + qi * jnp.where(lo256, -sx, sx)) + conv[:, 0:128]
        res[rows] = r.astype(BF16)

    for v in range(8):
        r = res[128 * v : 128 * v + 128].astype(F32)
        sr = swap(r)
        y[256 * v : 256 * v + 128, 0:128] = r.astype(BF16)
        y[256 * v + 128 : 256 * v + 256, 0:128] = jnp.where(lo, sr, -sr).astype(BF16)
    for m in range(4):
        rows = slice(256 * m, 256 * m + 256)
        corr = jnp.dot(w[rows], y[:, 0:128], preferred_element_type=F32)
        r = res[rows].astype(F32)
        sr = swap(r)
        g = (corr - (qr * r + qi * jnp.where(lo256, sr, -sr))) * (1.0 / 32.0)
        gs[rows] = g.astype(BF16)

        def send_back(i, carry):
            to = 8 * m + i
            pltpu.make_async_remote_copy(
                src_ref=gs.at[pl.ds(pl.multiple_of(to * 32, 32), 32)],
                dst_ref=got.at[part, xy],
                send_sem=gsend,
                recv_sem=grecv,
                device_id=(to, far_f),
                device_id_type=MESH,
            ).start()
            return carry

        lax.fori_loop(0, 8, send_back, 0)

    @pl.when(kept)
    def _():
        sent = zb.at[pl.ds(0, 992)]
        pltpu.make_async_copy(sent, sent, zsend).wait()

    pltpu.make_async_copy(xs, xs, xsend).wait()
    for axis in range(2):
        _, size, half = spans[axis]
        for count, part_size in ((10, size), (10, half)):
            for i in range(count):
                rows = pk.at[0, pl.ds(0, part_size)]
                pltpu.make_async_copy(rows, rows, psend).wait()
    pltpu.make_async_copy(gs, gs, gsend).wait()
    pltpu.make_async_copy(got, got, grecv).wait()


def unpack(got, out):
    lo = low_half(32)
    for a in range(2):
        for m in range(8):
            left, right = got[a, 2 * m].astype(F32), got[a, 2 * m + 1].astype(F32)
            out[0, a, :, 128 * m : 128 * m + 128] = jnp.where(lo, left, swap(right))
            out[1, a, :, 128 * m : 128 * m + 128] = jnp.where(lo, swap(left), right)


def body(traces, mute, operator, wavelet):
    table = jnp.asarray(band_table(1024, 32))
    vmem = pl.BlockSpec(memory_space=pltpu.VMEM)
    dma = pltpu.SemaphoreType.DMA
    got = pl.pallas_call(
        kernel,
        out_shape=jax.ShapeDtypeStruct((2, 16, 32, 128), BF16),
        in_specs=[vmem, pl.BlockSpec(memory_space=pl.ANY), vmem, vmem, pl.BlockSpec(memory_space=pltpu.SMEM)],
        out_specs=vmem,
        scratch_shapes=[
            pltpu.VMEM((32, 64, 1024), BF16),
            pltpu.VMEM((1024, 128), F32),
            pltpu.VMEM((1024, 128), BF16),
            pltpu.VMEM((18, 32, 128), BF16),
            pltpu.VMEM((16, 18, 32, 128), BF16),
            pltpu.VMEM((2, 16, 32, 128), BF16),
            pltpu.VMEM((1024, 128), BF16),
            pltpu.VMEM((1024, 2048), BF16),
            pltpu.VMEM((2048, 256), BF16),
            pltpu.VMEM((1024, 128), BF16),
            pltpu.VMEM((1024, 128), BF16),
            dma((4,)), dma, dma, dma, dma, dma, dma, dma, dma((40,)),
        ],
        compiler_params=pltpu.CompilerParams(
            collective_id=0, has_side_effects=True, vmem_limit_bytes=40 * 1024 * 1024
        ),
        cost_estimate=pl.CostEstimate(flops=1 << 30, bytes_accessed=5 << 20, transcendentals=0),
        name="evaluate",
    )(table, traces, mute, operator, wavelet)
    return pl.pallas_call(
        unpack,
        out_shape=jax.ShapeDtypeStruct((2, 2, 32, 1024), F32),
        in_specs=[vmem],
        out_specs=vmem,
        name="unpack",
    )(got)


def solution(mesh):
    in_specs = (P("blk", "freq", None), P("blk", "freq"), P(None, "freq", "blk", None), P())
    out_specs = P(None, "freq", "blk", None)
    return jax.shard_map(body, mesh=mesh, in_specs=in_specs, out_specs=out_specs, check_vma=False)
```

time: 547 us -> 79.3 us (0.14)
  the two profiles are of different devices: /device:TPU:96 before, /device:TPU:64 now
where the time goes in v1:
time: 79.3 us; the launch traced here: 79 us
  Pallas kernels  72.9 us (92%)
  local copies, waits for them, and re-layouts  6.13 us (8%)
    pallas_call x1, Pallas kernels, body(): pl.pallas_call(kernel, out_shape=jax.ShapeDtypeStruct((2, 16, 32, 128), B...  71 us
    unnamed x12, local copies, waits for them, and re-layouts  6.13 us
    pallas_call x1, Pallas kernels, body(): pl.pallas_call(unpack, out_shape=jax.ShapeDtypeStruct((2, 2, 32, 1024), F...  1.88 us

profile of v1, /device:TPU:64, one launch (start us, length us, event | category | flops | bytes accessed | tf_op | source)
XLA Modules:
  0.0 79.0 jit_solution(16497202268048170957)
XLA Ops:
  0.0 0.0 copy-start
  0.0 2.2 %copy-done = bf16[32,64,1024]{2,1,0:T(8,128)(2,1)S(1)} copy-done((bf16[32,64,1024]{2,1,0:T(8,128)(2,1)S(1)}, bf16[32,64,1024]{2,1,0:T(8,128)(2,1)}, u32[]{:S(2)}) %copy-start) | copy-done | bytes 4194328
  2.2 0.0 copy-start.2
  2.2 0.9 %copy-done.2 = bf16[2,2,32,1024]{3,2,1,0:T(8,128)(2,1)S(1)} copy-done((bf16[2,2,32,1024]{3,2,1,0:T(8,128)(2,1)S(1)}, bf16[2,2,32,1024]{3,2,1,0:T(8,128)(2,1)}, u32[]{:S(2)}) %copy-start.2) | copy-done | bytes 262168
  3.1 0.0 copy-start.3
  3.1 0.9 %copy-done.3 = bf16[64,1024]{1,0:T(8,128)(2,1)S(1)} copy-done((bf16[64,1024]{1,0:T(8,128)(2,1)S(1)}, bf16[64,1024]{1,0:T(8,128)(2,1)}, u32[]{:S(2)}) %copy-start.3) | copy-done | bytes 131096
  4.0 0.0 copy-start.4
  4.0 0.7 copy-done.4
  4.8 0.0 copy-start.5
  4.8 0.7 copy-done.5
  5.4 71.0 %evaluate.1.got = bf16[2,16,32,128]{3,2,1,0:T(8,128)(2,1)S(1)} custom-call(bf16[64,1024]{1,0:T(8,128)(2,1)S(1)} %copy-done.3, bf16[32,64,1024]{2,1,0:T(8,128)(2,1)S(1)} %copy-done, s32[32,64]{1,0:T(8,128)S(1)} %copy-done.4, bf16[2,2,32,1024]{3,2,1,0:T(8,128)(2,1)S(1)} %copy-done.2, f32[2,32]{1,0:T(2,128)S(1)} %copy-done.5), custom_call_target="tpu_custom_call" | custom-call | flops 1073741824 | bytes 5242880 | tf_op jit(solution)/shard_map/evaluate/pallas_call | solution.py:336
  76.4 0.0 copy-start.1
  76.4 0.7 copy-done.1
  77.1 1.9 %unpack.1 = f32[2,2,32,1024]{3,2,1,0:T(8,128)} custom-call(bf16[2,16,32,128]{3,2,1,0:T(8,128)(2,1)} %copy-done.1), custom_call_target="tpu_custom_call" | custom-call | tf_op jit(solution)/shard_map/unpack/pallas_call | solution.py:361
Async XLA Ops:
  0.0 2.2 %copy-start = (bf16[32,64,1024]{2,1,0:T(8,128)(2,1)S(1)}, bf16[32,64,1024]{2,1,0:T(8,128)(2,1)}, u32[]{:S(2)}) copy-start(bf16[32,64,1024]{2,1,0:T(8,128)(2,1)} %traces.1) | copy-start | bytes 12582916
  2.2 0.9 %copy-start.2 = (bf16[2,2,32,1024]{3,2,1,0:T(8,128)(2,1)S(1)}, bf16[2,2,32,1024]{3,2,1,0:T(8,128)(2,1)}, u32[]{:S(2)}) copy-start(bf16[2,2,32,1024]{3,2,1,0:T(8,128)(2,1)} %oper.1) | copy-start | bytes 786436
  3.1 0.9 %copy-start.3 = (bf16[64,1024]{1,0:T(8,128)(2,1)S(1)}, bf16[64,1024]{1,0:T(8,128)(2,1)}, u32[]{:S(2)}) copy-start(bf16[64,1024]{1,0:T(8,128)(2,1)} %constant.2.clone.table) | copy-start | bytes 393220
  4.0 0.7 copy-start.4
  4.8 0.7 copy-start.5
  76.4 0.7 copy-start.1

commit v2 on v1

v2 whole, which is shorter than its diff:
```python
import functools
import math

import jax
import jax.numpy as jnp
import numpy as np
from jax import lax
from jax.experimental import pallas as pl
from jax.experimental.pallas import tpu as pltpu
from jax.sharding import PartitionSpec as P

LOW_FREQ = 8
MESH = pl.DeviceIdType.MESH
BF16 = jnp.bfloat16
F32 = jnp.float32

OFFSETS = (0, 1, 3, 6, 4)


def div(a, b):
    return lax.div(a, jnp.int32(b))


def rem(a, b):
    return lax.rem(a, jnp.int32(b))


def wrap(a, n):
    return jnp.where(a >= n, a - n, a)


def frequency_at(device):
    z, core = device // 2, device % 2
    return (z % 8 + 4) % 8 * 4 + core * 2 + (1 + z // 8 + z % 8 // 4) % 2


def band_table(samples, count):
    times = np.arange(samples, dtype=np.int64)
    freqs = LOW_FREQ + np.array([frequency_at(t) for t in range(count)], dtype=np.int64)
    phase = times[:, None] * freqs[None, :] % samples
    angle = phase.astype(np.float32) * np.float32(2.0 * math.pi / samples)
    factor = np.float32(1.0 / math.sqrt(samples))
    table = np.concatenate([np.cos(angle) * factor, -np.sin(angle) * factor], axis=1)
    return np.ascontiguousarray(table.T).astype(jnp.bfloat16)


def swap(x):
    return pltpu.roll(x, 64, 1)


def low_half(rows):
    return lax.broadcasted_iota(jnp.int32, (rows, 128), 1) < 64


def kernel(
    table_in, traces, mute_in, oper_in, wave_in, got,
    table, mute, oper, wave, tr, zs, zb, pin, mid, pk, xs, xp, w, y, res, gs,
    in_sem, tr_sem, zsend, zrecv, xsend, xrecv, gsend, grecv, asend, arecv, bsend, brecv, csend, crecv,
):
    b = lax.axis_index("blk").astype(jnp.int32)
    f = lax.axis_index("freq").astype(jnp.int32)
    h, xy = div(b, 16), rem(b, 16)
    yy, xx = div(xy, 4), rem(xy, 4)
    l, core = div(f, 2), rem(f, 2)
    z = h * 8 + l
    u = h * 4 + yy
    d = rem(l - u + 8, 8)
    kept = (d == 0) | (d == 1) | (d == 3) | (d == 6) | ((d == 4) & (h == 0))
    slot = jnp.where(d == 1, 1, 0) + jnp.where(d == 3, 2, 0) + jnp.where(d == 6, 3, 0) + jnp.where(d == 4, 4, 0) + 5 * h
    far = rem(l + 4, 8)
    part = rem(1 + h + div(l, 4), 2)
    group = div(xx, 2)
    mine = far * 4 + group * 2 + part
    block = (yy * 2 + rem(xx, 2)) * 2 + core
    far_group = far * 2 + group

    def load(ch):
        return pltpu.make_async_copy(traces.at[pl.ds(8 * ch, 8)], tr.at[pl.ds(8 * ch, 8)], tr_sem.at[ch])

    @pl.when(kept)
    def _():
        load(0).start()

    inputs = [
        pltpu.make_async_copy(src, dst, in_sem.at[i])
        for i, (src, dst) in enumerate(((mute_in, mute), (table_in, table), (oper_in, oper), (wave_in, wave)))
    ]
    for c in inputs:
        c.start()

    @pl.when(kept)
    def _():
        for ch in range(1, 4):
            load(ch).start()

    barrier = pltpu.get_barrier_semaphore()

    def ring_device(to):
        return xy + jnp.where(to >= 8, 16, 0), wrap(to, 8) * 2 + core

    for half in range(2):
        for off in OFFSETS[: 5 - half]:
            to = 8 * half + wrap(yy + (4 * half + off) % 8, 8)

            @pl.when(to != z)
            def _():
                pl.semaphore_signal(barrier, inc=1, device_id=ring_device(to), device_id_type=MESH)

    at_y = [wrap(yy + i, 4) * 4 for i in range(4)]
    at_x = [wrap(xx + i, 4) for i in range(4)]

    def greet(device):
        pl.semaphore_signal(barrier, inc=1, device_id=device, device_id_type=MESH)

    def greet_far(i, carry):
        for half in range(2):
            for xl in range(2):
                to = 16 * half + 4 * i + xl
                greet((to + 2 * core, far * 2))
                greet((to + 2 * core, far * 2 + 1))
                greet((to + 2 - 2 * core, far_group))
        return carry

    lax.fori_loop(0, 4, greet_far, 0)

    def near(dy, dx, to_core):
        return h * 16 + at_y[dy] + at_x[dx], l * 2 + to_core

    greet(near(0, 0, 1 - core))
    for i in range(1, 4):
        greet(near(0, i, core))
        greet(near(i, 0, core))

    lo32 = low_half(32)
    for c in inputs:
        c.wait()
    for a in range(2):
        for m in range(8):
            re = oper[0, a, :, 128 * m : 128 * m + 128].astype(F32)
            im = oper[1, a, :, 128 * m : 128 * m + 128].astype(F32)
            xs[a, 2 * m] = jnp.where(lo32, re, swap(im)).astype(BF16)
            xs[a, 2 * m + 1] = jnp.where(lo32, swap(re), im).astype(BF16)

    @pl.when(kept)
    def _():
        eye = (lax.broadcasted_iota(jnp.int32, (64, 64), 0) == lax.broadcasted_iota(jnp.int32, (64, 64), 1)).astype(F32)
        ones = jnp.ones((64, 128), BF16)
        lane = lax.broadcasted_iota(jnp.int32, (512, 128), 1).astype(F32)
        for ch in range(4):
            starts = [
                (eye * mute[8 * ch + s : 8 * ch + s + 1, :].astype(F32)).astype(BF16) for s in range(8)
            ]
            first = jnp.dot(jnp.concatenate(starts, axis=0), ones, preferred_element_type=F32)
            load(ch).wait()
            head = tr[8 * ch : 8 * ch + 8, :, 0:128].astype(F32).reshape(512, 128)
            head = jnp.where(lane >= first, head, 0.0).astype(BF16)
            tr[8 * ch : 8 * ch + 8, :, 0:128] = head.reshape(8, 64, 128)
            spec = lax.dot_general(
                table[...], tr[8 * ch : 8 * ch + 8].reshape(512, 1024), (((1,), (1,)), ((), ())),
                preferred_element_type=F32,
            )
            for p in range(4):
                re = spec[0:32, 128 * p : 128 * p + 128]
                im = spec[32:64, 128 * p : 128 * p + 128]
                even = jnp.where(lo32, re, swap(im))
                odd = jnp.where(lo32, swap(re), im)
                s = 8 * ch + 2 * p
                for jt in range(4):
                    zs[pl.ds(jt * 256 + s, 8, stride=32), :] = even[8 * jt : 8 * jt + 8]
                    zs[pl.ds(jt * 256 + s + 1, 8, stride=32), :] = odd[8 * jt : 8 * jt + 8]
        zb[...] = zs[...].astype(BF16).reshape(32, 32, 128)

    @pl.when(kept)
    def _():
        pl.semaphore_wait(barrier, 70)

    @pl.when(jnp.logical_not(kept))
    def _():
        pl.semaphore_wait(barrier, 55)


    @pl.when(kept)
    def _():
        def send(to):
            pltpu.make_async_remote_copy(
                src_ref=zb.at[pl.ds(2 * to, 2)], dst_ref=pin.at[:, slot], send_sem=zsend, recv_sem=zrecv,
                device_id=ring_device(to), device_id_type=MESH,
            ).start()

        def send_two(i, carry):
            send(wrap(z + 7 - i, 16))
            send(wrap(z + 9 + i, 16))
            return carry

        send(wrap(z + 8, 16))
        lax.fori_loop(0, 7, send_two, 0)
        pltpu.make_async_copy(zb.at[pl.ds(2 * z, 2)], pin.at[:, slot], zrecv).start()

    to_half = [16 * rem(a + 1 + div(far, 4), 2) for a in range(2)]

    def send_oper():
        for i in range(4):
            for xl in range(2):
                for k in range(2):
                    for a in range(2):
                        pltpu.make_async_remote_copy(
                            src_ref=xs.at[a, at_y[i] + 2 * xl + k],
                            dst_ref=xp.at[pl.ds(pl.multiple_of(b * 32, 32), 32)],
                            send_sem=xsend,
                            recv_sem=xrecv,
                            device_id=(to_half[a] + at_y[i] + 2 * core + xl, far * 2 + k),
                            device_id_type=MESH,
                        ).start()

    def move(src, dst, send_sem, recv_sem, device):
        pltpu.make_async_remote_copy(
            src_ref=src, dst_ref=dst, send_sem=send_sem, recv_sem=recv_sem, device_id=device, device_id_type=MESH
        ).start()

    def arrived(ref, sem):
        pltpu.make_async_copy(ref, ref, sem).wait()

    def to_group(src, dst, send_sem, recv_sem):
        for which in range(2):
            for xl in range(2):
                to_x = 2 * which + xl

                @pl.when(xx != to_x)
                def _():
                    move(src.at[which], dst, send_sem, recv_sem, (h * 16 + at_y[0] + to_x, f))

                @pl.when(xx == to_x)
                def _():
                    pltpu.make_async_copy(src.at[which], dst, recv_sem).start()

    def fill(k):
        for row in range(8):
            for n in range(5 - row // 4):
                col = (row + OFFSETS[n]) % 8
                tile = jnp.concatenate([pk[row % 4, k, x, n + 5 * (row // 4)] for x in range(4)], axis=0)
                for c in range(2):
                    at = 256 * col + 128 * c + 64 * k
                    w[128 * row : 128 * row + 128, at : at + 64] = tile[:, 64 * c : 64 * c + 64]
                if col != row:
                    turned = tile.T
                    for c in range(2):
                        w[128 * col + 64 * k : 128 * col + 64 * k + 64, 256 * row + 128 * c : 256 * row + 128 * c + 128] = (
                            turned[64 * c : 64 * c + 64]
                        )

    arrived(pin, zrecv)

    @pl.when(core == 0)
    def _():
        to_group(pin, pk.at[yy, 0, xx], asend, arecv.at[yy, xx])
        for i in (2, 1, 3):
            move(pin.at[group], pk.at[yy, 0, xx], asend, arecv.at[yy, xx], near(i, 0, 0))

    @pl.when(core == 1)
    def _():
        for i in (2, 1, 3):
            move(pin, mid.at[yy], bsend, brecv.at[yy], near(i, 0, 1))
        to_group(pin, pk.at[yy, 1, xx], asend, arecv.at[yy, xx])

    send_oper()
    def pass_on(row, k):
        for x in range(4):
            arrived(pk.at[row, k, x], arecv.at[row, x])
        rows = pk.at[row, k]
        move(rows, rows, csend, crecv.at[row], near(0, 0, 1 - k))

    others = [div(at_y[i], 4) for i in (1, 3, 2)]

    @pl.when(core == 0)
    def _():
        for n in (1, 3, 2):
            x = at_x[n]
            panel = pk.at[yy, 0, x]
            arrived(panel, arecv.at[yy, x])
            for i in (2, 1, 3):
                move(panel, panel, asend, arecv.at[yy, x], near(i, 0, 0))
        arrived(pk.at[yy, 0, xx], arecv.at[yy, xx])
        move(pk.at[yy, 0], pk.at[yy, 0], csend, crecv.at[yy], near(0, 0, 1))
        for row in others:
            pass_on(row, 0)
        fill(0)
        for row in range(4):
            arrived(pk.at[row, 1], crecv.at[row])
        fill(1)

    @pl.when(core == 1)
    def _():
        for row in others:
            arrived(mid.at[row], brecv.at[row])
            to_group(mid.at[row], pk.at[row, 1, xx], asend, arecv.at[row, xx])
        for row in [yy, *others]:
            pass_on(row, 1)
        fill(1)
        for row in range(4):
            arrived(pk.at[row, 0], crecv.at[row])
        fill(0)

    pltpu.make_async_copy(xp, xp, xrecv).wait()
    lo = low_half(128)
    lane = lax.broadcasted_iota(jnp.int32, (128, 128), 1)
    row_at = lax.broadcasted_iota(jnp.int32, (128, 128), 0)
    for v in range(8):
        x = xp[128 * v : 128 * v + 128].astype(F32)
        sx = swap(x)
        y[256 * v : 256 * v + 128, 0:128] = x.astype(BF16)
        y[256 * v + 128 : 256 * v + 256, 0:128] = jnp.where(lo, -sx, sx).astype(BF16)
        here = row_at + (128 * v - 64 * block)
        y[256 * v : 256 * v + 128, 128:256] = jnp.where(lo & (lane == here), 1.0, 0.0).astype(BF16)
        y[256 * v + 128 : 256 * v + 256, 128:256] = jnp.where(
            (lane >= 64) & (lane - 64 == here), 1.0, 0.0
        ).astype(BF16)
    qr, qi = wave[0, mine], wave[1, mine]
    lo256 = low_half(256)
    for m in range(4):
        rows = slice(256 * m, 256 * m + 256)
        conv = jnp.dot(w[rows], y[...], preferred_element_type=F32)
        x = xp[rows].astype(F32)
        sx = swap(x)
        r = conv[:, 128:256] - (qr * x + qi * jnp.where(lo256, -sx, sx)) + conv[:, 0:128]
        res[rows] = r.astype(BF16)

    for v in range(8):
        r = res[128 * v : 128 * v + 128].astype(F32)
        sr = swap(r)
        y[256 * v : 256 * v + 128, 0:128] = r.astype(BF16)
        y[256 * v + 128 : 256 * v + 256, 0:128] = jnp.where(lo, sr, -sr).astype(BF16)
    for half in range(2):
        for at in (512 * half, 512 * half + 256):
            rows = slice(at, at + 256)
            corr = jnp.dot(w[rows], y[:, 0:128], preferred_element_type=F32)
            r = res[rows].astype(F32)
            sr = swap(r)
            g = (corr - (qr * r + qi * jnp.where(lo256, sr, -sr))) * (1.0 / 32.0)
            gs[rows] = g.astype(BF16)

        def send_back(i, carry):
            to = 16 * half + wrap(xy + i, 16)
            pltpu.make_async_remote_copy(
                src_ref=gs.at[pl.ds(pl.multiple_of(to * 32, 32), 32)],
                dst_ref=got.at[part, block],
                send_sem=gsend,
                recv_sem=grecv,
                device_id=(to, far_group),
                device_id_type=MESH,
            ).start()
            return carry

        lax.fori_loop(0, 16, send_back, 0)

    @pl.when(kept)
    def _():
        sent = zb.at[pl.ds(0, 30)]
        pltpu.make_async_copy(sent, sent, zsend).wait()

    pltpu.make_async_copy(xs, xs, xsend).wait()
    def left(ref, sem, times):
        for _ in range(times):
            pltpu.make_async_copy(ref, ref, sem).wait()

    left(pin.at[0], asend, 12)
    left(pk.at[0, 0], csend, 4)

    @pl.when(core == 0)
    def _():
        left(pin.at[0], asend, 3)

    @pl.when(core == 1)
    def _():
        left(pin, bsend, 3)

    pltpu.make_async_copy(gs, gs, gsend).wait()
    pltpu.make_async_copy(got, got, grecv).wait()


def unpack(got, out):
    lo = low_half(32)
    for a in range(2):
        for m in range(8):
            left, right = got[a, 2 * m].astype(F32), got[a, 2 * m + 1].astype(F32)
            out[0, a, :, 128 * m : 128 * m + 128] = jnp.where(lo, left, swap(right))
            out[1, a, :, 128 * m : 128 * m + 128] = jnp.where(lo, swap(left), right)


def body(traces, mute, operator, wavelet):
    table = jnp.asarray(band_table(1024, 32))
    vmem = pl.BlockSpec(memory_space=pltpu.VMEM)
    dma = pltpu.SemaphoreType.DMA
    got = pl.pallas_call(
        kernel,
        out_shape=jax.ShapeDtypeStruct((2, 16, 32, 128), BF16),
        in_specs=[pl.BlockSpec(memory_space=pltpu.HBM)] * 5,
        out_specs=vmem,
        scratch_shapes=[
            pltpu.VMEM((64, 1024), BF16),
            pltpu.VMEM((32, 64), jnp.int32),
            pltpu.VMEM((2, 2, 32, 1024), BF16),
            pltpu.SMEM((2, 32), F32),
            pltpu.VMEM((32, 64, 1024), BF16),
            pltpu.VMEM((1024, 128), F32),
            pltpu.VMEM((32, 32, 128), BF16),
            pltpu.VMEM((2, 9, 32, 128), BF16),
            pltpu.VMEM((4, 2, 9, 32, 128), BF16),
            pltpu.VMEM((4, 2, 4, 9, 32, 128), BF16),
            pltpu.VMEM((2, 16, 32, 128), BF16),
            pltpu.VMEM((1024, 128), BF16),
            pltpu.VMEM((1024, 2048), BF16),
            pltpu.VMEM((2048, 256), BF16),
            pltpu.VMEM((1024, 128), BF16),
            pltpu.VMEM((1024, 128), BF16),
            dma((4,)), dma((4,)), dma, dma, dma, dma, dma, dma,
            dma, dma((4, 4)), dma, dma((4,)), dma, dma((4,)),
        ],
        compiler_params=pltpu.CompilerParams(
            collective_id=0, has_side_effects=True, vmem_limit_bytes=56 * 1024 * 1024
        ),
        cost_estimate=pl.CostEstimate(flops=1 << 30, bytes_accessed=5 << 20, transcendentals=0),
        name="evaluate",
    )(table, traces, mute, operator, wavelet)
    return pl.pallas_call(
        unpack,
        out_shape=jax.ShapeDtypeStruct((2, 2, 32, 1024), F32),
        in_specs=[vmem],
        out_specs=vmem,
        name="unpack",
    )(got)


def solution(mesh):
    in_specs = (P("blk", "freq", None), P("blk", "freq"), P(None, "freq", "blk", None), P())
    out_specs = P(None, "freq", "blk", None)
    return jax.shard_map(body, mesh=mesh, in_specs=in_specs, out_specs=out_specs, check_vma=False)
```

time: 79.3 us -> 67.3 us (0.85)
  the two profiles are of different devices: /device:TPU:64 before, /device:TPU:1 now
where the time goes in v2:
time: 67.3 us; the launch traced here: 67.2 us
  Pallas kernels  67.2 us (100%)
    pallas_call x1, Pallas kernels, body(): pl.pallas_call(kernel, out_shape=jax.ShapeDtypeStruct((2, 16, 32, 128), B...  65.3 us
    pallas_call x1, Pallas kernels, body(): pl.pallas_call(unpack, out_shape=jax.ShapeDtypeStruct((2, 2, 32, 1024), F...  1.88 us

profile of v2, /device:TPU:1, one launch (start us, length us, event | category | flops | bytes accessed | tf_op | source)
XLA Modules:
  0.0 67.2 jit_solution(4028940641509149683)
XLA Ops:
  0.0 65.3 %evaluate.1.got = bf16[2,16,32,128]{3,2,1,0:T(8,128)(2,1)} custom-call(bf16[64,1024]{1,0:T(8,128)(2,1)} %constant.2.clone.table_in, bf16[32,64,1024]{2,1,0:T(8,128)(2,1)} %traces.1, s32[32,64]{1,0:T(8,128)} %mute_in.1, bf16[2,2,32,1024]{3,2,1,0:T(8,128)(2,1)} %oper_in.1, f32[2,32]{1,0:T(2,128)} %wave_in.1), custom_call_target="tpu_custom_call" | custom-call | flops 1073741824 | bytes 5242880 | tf_op jit(solution)/shard_map/evaluate/pallas_call | solution.py:393
  65.3 1.9 %unpack.1 = f32[2,2,32,1024]{3,2,1,0:T(8,128)} custom-call(bf16[2,16,32,128]{3,2,1,0:T(8,128)(2,1)} %evaluate.1.got), custom_call_target="tpu_custom_call" | custom-call | tf_op jit(solution)/shard_map/unpack/pallas_call | solution.py:424

commit v3 on v2

--- a/solution.py
+++ b/solution.py
@@ -54,8 +54,8 @@
 
 def kernel(
     table_in, traces, mute_in, oper_in, wave_in, got,
-    table, mute, oper, wave, tr, zs, zb, pin, mid, pk, xs, xp, w, y, res, gs,
-    in_sem, tr_sem, zsend, zrecv, xsend, xrecv, gsend, grecv, asend, arecv, bsend, brecv, csend, crecv,
+    table, mute, oper, wave, tr, zs, zb, pin, mid, pk, xs, xm, xp, w, y, res, gs,
+    in_sem, tr_sem, zsend, zrecv, xsend, xrecv, ysend, yrecv, gsend, grecv, asend, arecv, bsend, brecv, csend, crecv,
 ):
     b = lax.axis_index("blk").astype(jnp.int32)
     f = lax.axis_index("freq").astype(jnp.int32)
@@ -118,7 +118,6 @@
                 to = 16 * half + 4 * i + xl
                 greet((to + 2 * core, far * 2))
                 greet((to + 2 * core, far * 2 + 1))
-                greet((to + 2 - 2 * core, far_group))
         return carry
 
     lax.fori_loop(0, 4, greet_far, 0)
@@ -126,6 +125,16 @@
     def near(dy, dx, to_core):
         return h * 16 + at_y[dy] + at_x[dx], l * 2 + to_core
 
+    def greet_plane(i, carry):
+        @pl.when((i != xy) | (core != group))
+        def _():
+            greet((h * 16 + i, l * 2 + group))
+
+        return carry
+
+    lax.fori_loop(0, 16, greet_plane, 0)
+    for half in range(2):
+        greet((16 * half + xy, far * 2 + core))
     greet(near(0, 0, 1 - core))
     for i in range(1, 4):
         greet(near(0, i, core))
@@ -138,8 +147,8 @@
         for m in range(8):
             re = oper[0, a, :, 128 * m : 128 * m + 128].astype(F32)
             im = oper[1, a, :, 128 * m : 128 * m + 128].astype(F32)
-            xs[a, 2 * m] = jnp.where(lo32, re, swap(im)).astype(BF16)
-            xs[a, 2 * m + 1] = jnp.where(lo32, swap(re), im).astype(BF16)
+            xs[2 * m, a] = jnp.where(lo32, re, swap(im)).astype(BF16)
+            xs[2 * m + 1, a] = jnp.where(lo32, swap(re), im).astype(BF16)
 
     @pl.when(kept)
     def _():
@@ -170,14 +179,7 @@
                     zs[pl.ds(jt * 256 + s + 1, 8, stride=32), :] = odd[8 * jt : 8 * jt + 8]
         zb[...] = zs[...].astype(BF16).reshape(32, 32, 128)
 
-    @pl.when(kept)
-    def _():
-        pl.semaphore_wait(barrier, 70)
-
-    @pl.when(jnp.logical_not(kept))
-    def _():
-        pl.semaphore_wait(barrier, 55)
-
+    pl.semaphore_wait(barrier, 57 - jnp.where(core == group, 1, 0) + jnp.where(kept, 15, 0))
 
     @pl.when(kept)
     def _():
@@ -198,19 +200,23 @@
 
     to_half = [16 * rem(a + 1 + div(far, 4), 2) for a in range(2)]
 
-    def send_oper():
-        for i in range(4):
-            for xl in range(2):
-                for k in range(2):
-                    for a in range(2):
-                        pltpu.make_async_remote_copy(
-                            src_ref=xs.at[a, at_y[i] + 2 * xl + k],
-                            dst_ref=xp.at[pl.ds(pl.multiple_of(b * 32, 32), 32)],
-                            send_sem=xsend,
-                            recv_sem=xrecv,
-                            device_id=(to_half[a] + at_y[i] + 2 * core + xl, far * 2 + k),
-                            device_id_type=MESH,
-                        ).start()
+    for i in range(4):
+        for xl in range(2):
+            for k in range(2):
+                to_x = 2 * core + xl
+                src = xs.at[at_y[i] + 2 * xl + k]
+                other = (to_x != xx) | (core != k) if i == 0 else core >= 0
+
+                @pl.when(other)
+                def _():
+                    pltpu.make_async_remote_copy(
+                        src_ref=src, dst_ref=xm.at[:, xy], send_sem=xsend, recv_sem=xrecv,
+                        device_id=(h * 16 + at_y[i] + to_x, l * 2 + k), device_id_type=MESH,
+                    ).start()
+
+                @pl.when(jnp.logical_not(other))
+                def _():
+                    pltpu.make_async_copy(src, xm.at[:, xy], xrecv).start()
 
     def move(src, dst, send_sem, recv_sem, device):
         pltpu.make_async_remote_copy(
@@ -262,7 +268,13 @@
             move(pin, mid.at[yy], bsend, brecv.at[yy], near(i, 0, 1))
         to_group(pin, pk.at[yy, 1, xx], asend, arecv.at[yy, xx])
 
-    send_oper()
+    arrived(xm, xrecv)
+    for a in range(2):
+        move(
+            xm.at[a], xp.at[pl.ds(pl.multiple_of(16 * h, 16), 16)], ysend, yrecv,
+            (to_half[a] + xy, far * 2 + core),
+        )
+
     def pass_on(row, k):
         for x in range(4):
             arrived(pk.at[row, k, x], arecv.at[row, x])
@@ -300,12 +312,12 @@
             arrived(pk.at[row, 0], crecv.at[row])
         fill(0)
 
-    pltpu.make_async_copy(xp, xp, xrecv).wait()
+    pltpu.make_async_copy(xp, xp, yrecv).wait()
     lo = low_half(128)
     lane = lax.broadcasted_iota(jnp.int32, (128, 128), 1)
     row_at = lax.broadcasted_iota(jnp.int32, (128, 128), 0)
     for v in range(8):
-        x = xp[128 * v : 128 * v + 128].astype(F32)
+        x = xp[4 * v : 4 * v + 4].reshape(128, 128).astype(F32)
         sx = swap(x)
         y[256 * v : 256 * v + 128, 0:128] = x.astype(BF16)
         y[256 * v + 128 : 256 * v + 256, 0:128] = jnp.where(lo, -sx, sx).astype(BF16)
@@ -319,7 +331,7 @@
     for m in range(4):
         rows = slice(256 * m, 256 * m + 256)
         conv = jnp.dot(w[rows], y[...], preferred_element_type=F32)
-        x = xp[rows].astype(F32)
+        x = xp[8 * m : 8 * m + 8].reshape(256, 128).astype(F32)
         sx = swap(x)
         r = conv[:, 128:256] - (qr * x + qi * jnp.where(lo256, -sx, sx)) + conv[:, 0:128]
         res[rows] = r.astype(BF16)
@@ -357,7 +369,14 @@
         sent = zb.at[pl.ds(0, 30)]
         pltpu.make_async_copy(sent, sent, zsend).wait()
 
-    pltpu.make_async_copy(xs, xs, xsend).wait()
+    pltpu.make_async_copy(xm, xm, ysend).wait()
+    most = xs.at[pl.ds(0, 15)]
+    pltpu.make_async_copy(most, most, xsend).wait()
+
+    @pl.when(core != group)
+    def _():
+        pltpu.make_async_copy(xs.at[0], xs.at[0], xsend).wait()
+
     def left(ref, sem, times):
         for _ in range(times):
             pltpu.make_async_copy(ref, ref, sem).wait()
@@ -406,13 +425,14 @@
             pltpu.VMEM((2, 9, 32, 128), BF16),
             pltpu.VMEM((4, 2, 9, 32, 128), BF16),
             pltpu.VMEM((4, 2, 4, 9, 32, 128), BF16),
+            pltpu.VMEM((16, 2, 32, 128), BF16),
             pltpu.VMEM((2, 16, 32, 128), BF16),
-            pltpu.VMEM((1024, 128), BF16),
+            pltpu.VMEM((32, 32, 128), BF16),
             pltpu.VMEM((1024, 2048), BF16),
             pltpu.VMEM((2048, 256), BF16),
             pltpu.VMEM((1024, 128), BF16),
             pltpu.VMEM((1024, 128), BF16),
-            dma((4,)), dma((4,)), dma, dma, dma, dma, dma, dma,
+            dma((4,)), dma((4,)), dma, dma, dma, dma, dma, dma, dma, dma,
             dma, dma((4, 4)), dma, dma((4,)), dma, dma((4,)),
         ],
         compiler_params=pltpu.CompilerParams(

time: 67.3 us -> 65.2 us (0.969)
  Pallas kernels: 67.2 us -> 65 us
    pallas_call x1, Pallas kernels: 65.3 us -> 63.2 us  [body(): pl.pallas_call(kernel, out_shape=jax.ShapeDtypeStruct((2, 16, 32, 128), B...]
where the time goes in v3:
time: 65.2 us; the launch traced here: 65.1 us
  Pallas kernels  65 us (100%)
    pallas_call x1, Pallas kernels, body(): pl.pallas_call(kernel, out_shape=jax.ShapeDtypeStruct((2, 16, 32, 128), B...  63.2 us
    pallas_call x1, Pallas kernels, body(): pl.pallas_call(unpack, out_shape=jax.ShapeDtypeStruct((2, 2, 32, 1024), F...  1.88 us

profile of v3, /device:TPU:1, one launch (start us, length us, event | category | flops | bytes accessed | tf_op | source)
XLA Modules:
  0.0 65.1 jit_solution(9147908941942121506)
XLA Ops:
  0.0 63.2 %evaluate.1.got = bf16[2,16,32,128]{3,2,1,0:T(8,128)(2,1)} custom-call(bf16[64,1024]{1,0:T(8,128)(2,1)} %constant.2.clone.table_in, bf16[32,64,1024]{2,1,0:T(8,128)(2,1)} %traces.1, s32[32,64]{1,0:T(8,128)} %mute_in.1, bf16[2,2,32,1024]{3,2,1,0:T(8,128)(2,1)} %oper_in.1, f32[2,32]{1,0:T(2,128)} %wave_in.1), custom_call_target="tpu_custom_call" | custom-call | flops 1073741824 | bytes 5242880 | tf_op jit(solution)/shard_map/evaluate/pallas_call | solution.py:412
  63.2 1.9 %unpack.1 = f32[2,2,32,1024]{3,2,1,0:T(8,128)} custom-call(bf16[2,16,32,128]{3,2,1,0:T(8,128)(2,1)} %evaluate.1.got), custom_call_target="tpu_custom_call" | custom-call | tf_op jit(solution)/shard_map/unpack/pallas_call | solution.py:444

commit v4 on v3

--- a/solution.py
+++ b/solution.py
@@ -190,11 +190,24 @@
             ).start()
 
         def send_two(i, carry):
-            send(wrap(z + 7 - i, 16))
-            send(wrap(z + 9 + i, 16))
+            for to in (wrap(z + 7 - i, 16), wrap(z + 9 + i, 16)):
+
+                @pl.when((to != 4) & (to != 12))
+                def _():
+                    send(to)
+
             return carry
 
-        send(wrap(z + 8, 16))
+        for to in (4, 12):
+
+            @pl.when(z != to)
+            def _():
+                send(jnp.int32(to))
+
+        @pl.when((z != 4) & (z != 12))
+        def _():
+            send(wrap(z + 8, 16))
+
         lax.fori_loop(0, 7, send_two, 0)
         pltpu.make_async_copy(zb.at[pl.ds(2 * z, 2)], pin.at[:, slot], zrecv).start()
 
@@ -341,17 +354,16 @@
         sr = swap(r)
         y[256 * v : 256 * v + 128, 0:128] = r.astype(BF16)
         y[256 * v + 128 : 256 * v + 256, 0:128] = jnp.where(lo, sr, -sr).astype(BF16)
-    for half in range(2):
-        for at in (512 * half, 512 * half + 256):
-            rows = slice(at, at + 256)
-            corr = jnp.dot(w[rows], y[:, 0:128], preferred_element_type=F32)
-            r = res[rows].astype(F32)
-            sr = swap(r)
-            g = (corr - (qr * r + qi * jnp.where(lo256, sr, -sr))) * (1.0 / 32.0)
-            gs[rows] = g.astype(BF16)
+    for at in (0, 256, 512, 768):
+        rows = slice(at, at + 256)
+        corr = jnp.dot(w[rows], y[:, 0:128], preferred_element_type=F32)
+        r = res[rows].astype(F32)
+        sr = swap(r)
+        g = (corr - (qr * r + qi * jnp.where(lo256, sr, -sr))) * (1.0 / 32.0)
+        gs[rows] = g.astype(BF16)
 
         def send_back(i, carry):
-            to = 16 * half + wrap(xy + i, 16)
+            to = at // 32 + wrap(rem(xy, 8) + i, 8)
             pltpu.make_async_remote_copy(
                 src_ref=gs.at[pl.ds(pl.multiple_of(to * 32, 32), 32)],
                 dst_ref=got.at[part, block],
@@ -362,7 +374,7 @@
             ).start()
             return carry
 
-        lax.fori_loop(0, 16, send_back, 0)
+        lax.fori_loop(0, 8, send_back, 0)
 
     @pl.when(kept)
     def _():

time: 65.2 us -> 64.1 us (0.983)
  the two profiles are of different devices: /device:TPU:1 before, /device:TPU:129 now
where the time goes in v4:
time: 64.1 us; the launch traced here: 63.9 us
  Pallas kernels  63.9 us (100%)
    pallas_call x1, Pallas kernels, body(): pl.pallas_call(kernel, out_shape=jax.ShapeDtypeStruct((2, 16, 32, 128), B...  62.1 us
    pallas_call x1, Pallas kernels, body(): pl.pallas_call(unpack, out_shape=jax.ShapeDtypeStruct((2, 2, 32, 1024), F...  1.88 us

profile of v4, /device:TPU:129, one launch (start us, length us, event | category | flops | bytes accessed | tf_op | source)
XLA Modules:
  0.0 63.9 jit_solution(5616336483311477434)
XLA Ops:
  0.0 62.1 %evaluate.1.got = bf16[2,16,32,128]{3,2,1,0:T(8,128)(2,1)} custom-call(bf16[64,1024]{1,0:T(8,128)(2,1)} %constant.2.clone.table_in, bf16[32,64,1024]{2,1,0:T(8,128)(2,1)} %traces.1, s32[32,64]{1,0:T(8,128)} %mute_in.1, bf16[2,2,32,1024]{3,2,1,0:T(8,128)(2,1)} %oper_in.1, f32[2,32]{1,0:T(2,128)} %wave_in.1), custom_call_target="tpu_custom_call" | custom-call | flops 1073741824 | bytes 5242880 | tf_op jit(solution)/shard_map/evaluate/pallas_call | solution.py:424
  62.1 1.9 %unpack.1 = f32[2,2,32,1024]{3,2,1,0:T(8,128)} custom-call(bf16[2,16,32,128]{3,2,1,0:T(8,128)(2,1)} %evaluate.1.got), custom_call_target="tpu_custom_call" | custom-call | tf_op jit(solution)/shard_map/unpack/pallas_call | solution.py:456

commit v5 on v4

--- a/solution.py
+++ b/solution.py
@@ -177,7 +177,7 @@
                 for jt in range(4):
                     zs[pl.ds(jt * 256 + s, 8, stride=32), :] = even[8 * jt : 8 * jt + 8]
                     zs[pl.ds(jt * 256 + s + 1, 8, stride=32), :] = odd[8 * jt : 8 * jt + 8]
-        zb[...] = zs[...].astype(BF16).reshape(32, 32, 128)
+        zb[...] = zs[0:1024].astype(BF16).reshape(32, 32, 128)
 
     pl.semaphore_wait(barrier, 57 - jnp.where(core == group, 1, 0) + jnp.where(kept, 15, 0))
 
@@ -432,7 +432,7 @@
             pltpu.VMEM((2, 2, 32, 1024), BF16),
             pltpu.SMEM((2, 32), F32),
             pltpu.VMEM((32, 64, 1024), BF16),
-            pltpu.VMEM((1024, 128), F32),
+            pltpu.VMEM((1056, 128), F32),
             pltpu.VMEM((32, 32, 128), BF16),
             pltpu.VMEM((2, 9, 32, 128), BF16),
             pltpu.VMEM((4, 2, 9, 32, 128), BF16),

time: 64.1 us -> 64.1 us (level)
  no operation moved by 1% of the time
where the time goes in v5:
time: 64.1 us; the launch traced here: 63.9 us
  Pallas kernels  63.9 us (100%)
    pallas_call x1, Pallas kernels, body(): pl.pallas_call(kernel, out_shape=jax.ShapeDtypeStruct((2, 16, 32, 128), B...  62.1 us
    pallas_call x1, Pallas kernels, body(): pl.pallas_call(unpack, out_shape=jax.ShapeDtypeStruct((2, 2, 32, 1024), F...  1.88 us

profile of v5, /device:TPU:129, one launch (start us, length us, event | category | flops | bytes accessed | tf_op | source)
XLA Modules:
  0.0 63.9 jit_solution(3514268203904631965)
XLA Ops:
  0.0 62.1 %evaluate.1.got = bf16[2,16,32,128]{3,2,1,0:T(8,128)(2,1)} custom-call(bf16[64,1024]{1,0:T(8,128)(2,1)} %constant.2.clone.table_in, bf16[32,64,1024]{2,1,0:T(8,128)(2,1)} %traces.1, s32[32,64]{1,0:T(8,128)} %mute_in.1, bf16[2,2,32,1024]{3,2,1,0:T(8,128)(2,1)} %oper_in.1, f32[2,32]{1,0:T(2,128)} %wave_in.1), custom_call_target="tpu_custom_call" | custom-call | flops 1073741824 | bytes 5242880 | tf_op jit(solution)/shard_map/evaluate/pallas_call | solution.py:424
  62.1 1.9 %unpack.1 = f32[2,2,32,1024]{3,2,1,0:T(8,128)} custom-call(bf16[2,16,32,128]{3,2,1,0:T(8,128)(2,1)} %evaluate.1.got), custom_call_target="tpu_custom_call" | custom-call | tf_op jit(solution)/shard_map/unpack/pallas_call | solution.py:456
